TPU v7x, 32 devices: a whole 2x2x4 slice. The times are simulated.
32 devices in a mesh: sa: 8 (over z, core), sb: 4 (over y, x).
Axes of the slice: x: 2, y: 2, z: 4, core: 2. Of those that a mesh axis runs over, the one named last changes fastest.
Arguments:
- queries: bfloat16 [4096, 16, 192], P(('sa', 'sb')), may hold values from -110 to 110
- keys: bfloat16 [4096, 192], P(('sa', 'sb')), may hold values from -6 to 6
- values: bfloat16 [4096, 128], P(('sa', 'sb')), may hold values from -6 to 6
- key_first: bfloat16 [6144, 192], replicated, may hold values from -0.078125 to 0.078125
- key_second: bfloat16 [192, 192], replicated, may hold values from -0.4375 to 0.4375
- value_first: bfloat16 [4096, 128], replicated, may hold values from -0.09375 to 0.09375
- value_second: bfloat16 [128, 128], replicated, may hold values from -0.5 to 0.5
- gate_table: float32 [16, 2], replicated, may hold values from 0.1 to 1
- gate_index: int32 [4096, 16], P(('sa', 'sb')), may hold values from 0 to 15
Outputs:
- mixed: bfloat16 [4096, 16, 128], P(('sa', 'sb'))
All inputs are finite; a program needn't handle non-finite values.
Results may differ from a plain program's by a relative error of at most 0.0053.
Values may be sent and summed in bfloat16 or wider, within the bound.
A program may use at most 64 MiB of HBM per device.

v0:
```python
import jax
import jax.numpy as jnp
from jax import lax
from jax.sharding import PartitionSpec as P

STRIDE = 16
WINDOW = 512


span_cols = 512


def shifted(shard, axis, by):
    size = lax.axis_size(axis)
    pairs = [(i, i + by) for i in range(size) if 0 <= i + by < size]
    return lax.ppermute(shard, axis, pairs)


def summarize(padded, first, second, count):
    width = padded.shape[1]
    front = padded[: count * STRIDE].reshape(count, STRIDE * width)
    back = padded[STRIDE:].reshape(count, STRIDE * width)
    flat = jnp.concatenate([front, back], axis=1)
    hidden = jax.nn.silu(jnp.dot(flat, first, preferred_element_type=jnp.float32)).astype(
        jnp.bfloat16
    )
    return jnp.dot(hidden, second, preferred_element_type=jnp.float32).astype(jnp.bfloat16)


def local(
    queries, keys, values, key_first, key_second, value_first, value_second, gate_table, gate_index
):
    rows, heads, depth = queries.shape
    device = lax.axis_index(("sa", "sb"))
    reach = WINDOW // rows
    scale = depth ** (-0.5)
    paired = jnp.concatenate([keys, values], axis=1)
    earlier = []
    for distance in range(1, reach + 1):
        earlier.append(shifted(paired, ("sa", "sb"), distance))
    context = jnp.concatenate(earlier[::-1] + [paired], axis=0)
    padded = jnp.concatenate([earlier[0][rows - STRIDE :], paired], axis=0)
    count = rows // STRIDE
    key_summary = summarize(padded[:, :depth], key_first, key_second, count)
    value_summary = summarize(padded[:, depth:], value_first, value_second, count)
    query_rows = queries.reshape(rows * heads, depth)
    positions = device * rows + lax.iota(jnp.int32, rows * heads) // heads
    last_position = device * rows + rows - 1

    def absorb(carry, key_part, value_part, start):
        best, total, accum = carry
        length = key_part.shape[0]
        scores = (
            jnp.einsum("rd,nd->rn", query_rows, key_part, preferred_element_type=jnp.float32)
            * scale
        )
        ends = STRIDE * (start + lax.iota(jnp.int32, length)) + STRIDE - 1
        visible = ends[None, :] <= positions[:, None]
        masked = jnp.where(visible, scores, -1e30)
        fresh = jnp.maximum(best, jnp.max(masked, axis=1))
        weights = jnp.where(visible, jnp.exp(masked - fresh[:, None]), 0.0)
        shrink = jnp.exp(best - fresh)
        total = total * shrink + jnp.sum(weights, axis=1)
        accum = accum * shrink[:, None] + jnp.dot(
            weights.astype(jnp.bfloat16), value_part, preferred_element_type=jnp.float32
        )
        return (fresh, total, accum)

    grouped = (
        lax.all_gather(key_summary, "sb", axis=0, tiled=True),
        lax.all_gather(value_summary, "sb", axis=0, tiled=True),
    )
    all_keys, all_values = (
        lax.all_gather(grouped[0], "sa", axis=0, tiled=True),
        lax.all_gather(grouped[1], "sa", axis=0, tiled=True),
    )
    blocks = all_keys.shape[0]
    width_cols = min(span_cols, blocks)

    def inner(state, number):
        offset = number * width_cols

        def work(current):
            key_slice = lax.dynamic_slice_in_dim(all_keys, offset, width_cols, 0)
            value_slice = lax.dynamic_slice_in_dim(all_values, offset, width_cols, 0)
            return absorb(current, key_slice, value_slice, offset)

        def skipped(current):
            return current

        needed = STRIDE * offset + STRIDE - 1 <= last_position
        return (lax.cond(needed, work, skipped, state), None)

    initial = (
        jnp.full((rows * heads,), -1e30, jnp.float32),
        jnp.zeros((rows * heads,), jnp.float32),
        jnp.zeros((rows * heads, all_values.shape[1]), jnp.float32),
    )
    (best, total, accum), unused = lax.scan(
        inner, initial, jnp.arange(blocks // width_cols, dtype=jnp.int32)
    )
    present = total > 0.0
    compressed = jnp.where(present[:, None], accum / jnp.where(present, total, 1.0)[:, None], 0.0)
    near_keys = context[:, :depth]
    near_values = context[:, depth:]
    key_pos = (device - reach) * rows + lax.iota(jnp.int32, context.shape[0])
    near_scores = (
        jnp.einsum("rd,nd->rn", query_rows, near_keys, preferred_element_type=jnp.float32) * scale
    )
    inside = (
        (key_pos[None, :] <= positions[:, None])
        & (key_pos[None, :] > positions[:, None] - WINDOW)
        & (key_pos[None, :] >= 0)
    )
    near_masked = jnp.where(inside, near_scores, -1e30)
    near_top = jnp.max(near_masked, axis=1, keepdims=True)
    near_weights = jnp.where(inside, jnp.exp(near_masked - near_top), 0.0)
    near_total = jnp.sum(near_weights, axis=1)
    window = (
        jnp.dot(near_weights.astype(jnp.bfloat16), near_values, preferred_element_type=jnp.float32)
        / near_total[:, None]
    )
    chosen = gate_index.reshape(rows * heads)
    onehot = (chosen[:, None] == lax.iota(jnp.int32, gate_table.shape[0])[None, :]).astype(
        jnp.float32
    )
    gates = jnp.sum(onehot[:, :, None] * gate_table[None, :, :], axis=1)
    mixed = gates[:, 0:1] * compressed + gates[:, 1:2] * window
    return mixed.astype(jnp.bfloat16).reshape(rows, heads, all_values.shape[1])


def solution(mesh):
    in_specs = (
        P(("sa", "sb"), None, None),
        P(("sa", "sb"), None),
        P(("sa", "sb"), None),
        P(),
        P(),
        P(),
        P(),
        P(),
        P(("sa", "sb"), None),
    )
    out_specs = P(("sa", "sb"), None, None)
    return jax.shard_map(local, mesh=mesh, in_specs=in_specs, out_specs=out_specs, check_vma=False)
```

profile of v0, /device:TPU:0, one launch (start us, length us, event | category | flops | bytes accessed | tf_op | source)
XLA Modules:
  0.0 100.6 jit_solution(16138684351204684427)
XLA Ops:
  0.0 1.0 %copy.22 = bf16[128,128]{0,1:T(8,128)(2,1)S(1)} copy(bf16[128,128]{1,0:T(8,128)(2,1)} %param.13) | data formatting | bytes 65536 | tf_op args[2]
  1.0 1.4 %pad_maximum_fusion = bf16[128,320]{0,1:T(8,128)(2,1)} fusion(bf16[128,128]{0,1:T(8,128)(2,1)S(1)} %copy.22, bf16[128,192]{0,1:T(8,128)(2,1)} %param.12), kind=kLoop, calls=%fused_computation.43 | loop fusion | flops 163840 | bytes 163840 | tf_op jit(solution)/shard_map/concatenate | solution.py:37
  2.5 6.4 %collective-permute-start.2 = (bf16[128,320]{0,1:T(8,128)(2,1)}, bf16[128,320]{0,1:T(8,128)(2,1)}, u32[]{:S(2)}, u32[]{:S(2)}) collective-permute-start(bf16[128,320]{0,1:T(8,128)(2,1)} %pad_maximum_fusion), channel_id=1, source_target_pairs={{0,3},{1,4},{2,5},{3,6},{4,7},{5,8},{6,9},{7,10},{8,11},{9,12},{10... | collective-permute-start | bytes 245768 | tf_op jit(solution)/shard_map/ppermute | solution.py:16
  8.9 1.9 %collective-permute-start.1 = (bf16[128,320]{0,1:T(8,128)(2,1)}, bf16[128,320]{0,1:T(8,128)(2,1)}, u32[]{:S(2)}, u32[]{:S(2)}) collective-permute-start(bf16[128,320]{0,1:T(8,128)(2,1)} %pad_maximum_fusion), channel_id=1, source_target_pairs={{0,4},{1,5},{2,6},{3,7},{4,8},{5,9},{6,10},{7,11},{8,12},{9,13},{1... | collective-permute-start | bytes 245768 | tf_op jit(solution)/shard_map/ppermute | solution.py:16
  10.8 4.2 %collective-permute-start.3 = (bf16[128,320]{0,1:T(8,128)(2,1)}, bf16[128,320]{0,1:T(8,128)(2,1)}, u32[]{:S(2)}, u32[]{:S(2)}) collective-permute-start(bf16[128,320]{0,1:T(8,128)(2,1)} %pad_maximum_fusion), channel_id=1, source_target_pairs={{0,2},{1,3},{2,4},{3,5},{4,6},{5,7},{6,8},{7,9},{8,10},{9,11},{10,... | collective-permute-start | bytes 245768 | tf_op jit(solution)/shard_map/ppermute | solution.py:16
  15.0 3.1 %collective-permute-start = (bf16[128,320]{0,1:T(8,128)(2,1)}, bf16[128,320]{0,1:T(8,128)(2,1)}, u32[]{:S(2)}, u32[]{:S(2)}) collective-permute-start(bf16[128,320]{0,1:T(8,128)(2,1)} %pad_maximum_fusion), channel_id=1, source_target_pairs={{0,1},{1,2},{2,3},{3,4},{4,5},{5,6},{6,7},{7,8},{8,9},{9,10},{10,1... | collective-permute-start | bytes 245768 | tf_op jit(solution)/shard_map/ppermute | solution.py:16
  24.7 2.6 %copy.21 = bf16[128,16,192]{2,1,0:T(8,128)(2,1)} copy(bf16[128,16,192]{0,2,1:T(8,128)(2,1)} %param.11) | data formatting | bytes 1572864 | tf_op args[0]
  28.5 1.0 slice.39
  31.8 2.2 %convolution_convert_fusion.1 = bf16[8,128]{1,0:T(8,128)(2,1)} fusion(bf16[128,128]{1,0:T(8,128)(2,1)} %param.17, bf16[4096,128]{1,0:T(8,128)(2,1)} %param.16, bf16[8,2048]{1,0:T(8,128)(2,1)S(1)} %reshape.87, bf16[8,2048]{1,0:T(8,128)(2,1)S(1)} %reshape.86), kind=kOutput, calls=%fused_computation.32 | convolution fusion | flops 8787968 | bytes 1148928 | tf_op jit(solution)/shard_map/dot_general | solution.py:27
  34.0 8.3 %all_gather.14 = bf16[32,128]{1,0:T(8,128)(2,1)} all-gather(bf16[8,128]{1,0:T(8,128)(2,1)} %convolution_convert_fusion.1), channel_id=1, replica_groups=mesh['sa'=8,'sb'=4] {'sb'}, dimensions={0}, use_global_device_ids=true | all-gather | bytes 10240 | tf_op jit(solution)/shard_map/all_gather | solution.py:71
  44.0 1.8 %convolution_convert_fusion = bf16[8,192]{1,0:T(8,128)(2,1)S(1)} fusion(bf16[192,192]{1,0:T(8,128)(2,1)} %param.15, bf16[6144,192]{0,1:T(8,128)(2,1)S(1)} %copy-done, bf16[8,3072]{1,0:T(8,128)(2,1)} %reshape.85, bf16[8,3072]{1,0:T(8,128)(2,1)} %reshape.84), kind=kOutput, calls=%fused_computation.31 | convolution fusion | flops 19670016 | bytes 2534400 | tf_op jit(solution)/shard_map/dot_general | solution.py:27
  45.8 7.4 %all_gather.12 = bf16[32,192]{1,0:T(8,128)(2,1)S(1)} all-gather(bf16[8,192]{1,0:T(8,128)(2,1)S(1)} %convolution_convert_fusion), channel_id=1, replica_groups=mesh['sa'=8,'sb'=4] {'sb'}, dimensions={0}, use_global_device_ids=true | all-gather | bytes 15360 | tf_op jit(solution)/shard_map/all_gather | solution.py:70
  53.2 14.1 %all_gather.15 = bf16[256,128]{1,0:T(8,128)(2,1)S(1)} all-gather(bf16[32,128]{1,0:T(8,128)(2,1)S(1)} %copy-done.5), channel_id=1, replica_groups=mesh['sa'=8,'sb'=4] {'sa'}, dimensions={0}, use_global_device_ids=true | all-gather | bytes 73728 | tf_op jit(solution)/shard_map/all_gather | solution.py:75
  67.3 15.2 %all_gather.13 = bf16[256,192]{1,0:T(8,128)(2,1)} all-gather(bf16[32,192]{1,0:T(8,128)(2,1)S(1)} %all_gather.12), channel_id=1, replica_groups=mesh['sa'=8,'sb'=4] {'sa'}, dimensions={0}, use_global_device_ids=true | all-gather | bytes 110592 | tf_op jit(solution)/shard_map/all_gather | solution.py:74
  82.6 3.3 %conditional.1 = ((f32[2048]{0:T(1024)S(1)}, f32[2048,128]{1,0:T(8,128)S(1)})) conditional(s32[]{:T(128)} %convert_element_type.34, (f32[2048]{0:T(1024)S(1)}, f32[2048,128]{1,0:T(8,128)S(1)}) %tuple.31, (s32[]{:T(128)}, s32[2048]{0:T(1024)S(1)}, s32[2048]{0:T(1024)S(1)}, bf16[2048,192]{1,0:T(8,128)(2,1)}, bf16[256,192]{1,0:T(8,128)(2,1)}, ...), branch_computations={%region_1.2_spmd, %region_2.5_spmd} | conditional | flops 342383104 | bytes 9490460 | solution.py:92
  82.6 1.7 %fusion.63 = (f32[2048]{0:T(1024)S(1)}, f32[2048,256]{0,1:T(8,128)S(1)}) fusion(bf16[2048,192]{1,0:T(8,128)(2,1)} %get-tuple-element.95, bf16[256,192]{1,0:T(8,128)(2,1)} %get-tuple-element.96, s32[2048]{0:T(1024)S(1)} %fusion.8, s32[256]{0:T(256)S(1)} %multiply_add_fusion.1), kind=kOutput, calls=%fused_computation.80 | convolution fusion | flops 203421696 | bytes 2999296 | tf_op jit(solution)/shard_map/while/body/eval_jaxpr/cond/branch_1_fun/rd,nd->rn/dot_general | solution.py:54
  84.9 1.1 %convolution_add_fusion = f32[2048,128]{1,0:T(8,128)S(1)} fusion(bf16[256,128]{1,0:T(8,128)(2,1)S(1)} %get-tuple-element.98, f32[2048,256]{0,1:T(8,128)S(1)} %get-tuple-element.106, f32[2048,128]{1,0:T(8,128)S(1)} %get-tuple-element.97, f32[2048]{0:T(1024)S(1)} %broadcast_maximum_fusion, s32[2048]{0:T(1024)S(1)} %fusion.8, s32[256]{0:T(256)S(1)} %multiply_add_fusion.1, ...), kind=kOutput, calls=%fused_computation.3 | convolution fusion | flops 136839168 | bytes 4285440 | tf_op jit(solution)/shard_map/while/body/eval_jaxpr/cond/branch_1_fun/dot_general | solution.py:64
  86.0 0.9 constant_dynamic-update-slice_fusion.4
  86.9 0.9 constant_dynamic-update-slice_fusion.3
  87.8 0.9 constant_dynamic-update-slice_fusion.2
  88.7 0.9 constant_dynamic-update-slice_fusion.1
  89.7 3.8 %fusion.11 = (f32[2048]{0:T(1024)S(1)}, f32[640,2048]{1,0:T(8,128)S(1)}) fusion(pred[640]{0:T(1024)(128)(4,1)S(1)} %copy-done.10, s32[2048]{0:T(1024)S(1)} %copy-done.4, s32[2048]{0:T(1024)S(1)} %copy-done.3, s32[640]{0:T(1024)S(1)} %copy-done.7, bf16[2048,192]{1,0:T(8,128)(2,1)} %bitcast.32, bf16[640,320]{0,1:T(8,128)(2,1)S(1)} %constant_dynamic-update-slice_fusion), kind=kOutput, calls=%fused_computation.23 | convolution fusion | flops 512489472 | bytes 6304768 | tf_op jit(solution)/shard_map/rd,nd->rn/dot_general | solution.py:108
  93.5 2.6 %fusion.12 = f32[2048]{0:T(1024)S(1)} fusion(f32[640,2048]{1,0:T(8,128)S(1)} %get-tuple-element.110, f32[2048]{0:T(1024)S(1)} %get-tuple-element.109, pred[640]{0:T(1024)(128)(4,1)S(1)} %copy-done.10, s32[2048]{0:T(1024)S(1)} %copy-done.4, s32[2048]{0:T(1024)S(1)} %copy-done.3, s32[640]{0:T(1024)S(1)} %copy-done.7), kind=kLoop, calls=%fused_computation.24 | loop fusion | flops 11794432 | bytes 5278848 | tf_op jit(solution)/shard_map/reduce_sum | solution.py:118
  96.2 4.4 %fusion.25 = bf16[2048,128]{1,0:T(8,128)(2,1)} fusion(f32[640,2048]{1,0:T(8,128)S(1)} %get-tuple-element.110, f32[2048]{0:T(1024)S(1)} %get-tuple-element.109, f32[2048,128]{1,0:T(8,128)S(1)} %get-tuple-element.102, f32[2048]{0:T(1024)S(1)} %fusion.12, f32[2048]{0:T(1024)S(1)} %bitcast.34, f32[2048]{0:T(1024)S(1)} %broadcast_select_fusion, ...), kind=kOutput, calls=%fused_computation.30 | convolution fusion | flops 349175808 | bytes 7044096 | tf_op jit(solution)/shard_map/dot_general | solution.py:120
  (55 shorter events, 12.2 us)
Async XLA Ops:
  0.0 43.9 %copy-start = (bf16[6144,192]{0,1:T(8,128)(2,1)S(1)}, bf16[6144,192]{0,1:T(8,128)(2,1)}, u32[]{:S(2)}) copy-start(bf16[6144,192]{0,1:T(8,128)(2,1)} %param.14) | copy-start | bytes 7077892
  0.0 29.5 %copy-start.1 = (bf16[128,192]{0,1:T(8,128)(2,1)S(1)}, bf16[128,192]{0,1:T(8,128)(2,1)}, u32[]{:S(2)}) copy-start(bf16[128,192]{0,1:T(8,128)(2,1)} %param.12) | copy-start | bytes 147460
  2.5 84.4 %collective-permute-start.2 = (bf16[128,320]{0,1:T(8,128)(2,1)}, bf16[128,320]{0,1:T(8,128)(2,1)}, u32[]{:S(2)}, u32[]{:S(2)}) collective-permute-start(bf16[128,320]{0,1:T(8,128)(2,1)} %pad_maximum_fusion), channel_id=1, source_target_pairs={{0,3},{1,4},{2,5},{3,6},{4,7},{5,8},{6,9},{7,10},{8,11},{9,12},{10... | collective-permute-start | bytes 245768 | tf_op jit(solution)/shard_map/ppermute | solution.py:16
  8.9 77.1 %collective-permute-start.1 = (bf16[128,320]{0,1:T(8,128)(2,1)}, bf16[128,320]{0,1:T(8,128)(2,1)}, u32[]{:S(2)}, u32[]{:S(2)}) collective-permute-start(bf16[128,320]{0,1:T(8,128)(2,1)} %pad_maximum_fusion), channel_id=1, source_target_pairs={{0,4},{1,5},{2,6},{3,7},{4,8},{5,9},{6,10},{7,11},{8,12},{9,13},{1... | collective-permute-start | bytes 245768 | tf_op jit(solution)/shard_map/ppermute | solution.py:16
  10.8 77.0 %collective-permute-start.3 = (bf16[128,320]{0,1:T(8,128)(2,1)}, bf16[128,320]{0,1:T(8,128)(2,1)}, u32[]{:S(2)}, u32[]{:S(2)}) collective-permute-start(bf16[128,320]{0,1:T(8,128)(2,1)} %pad_maximum_fusion), channel_id=1, source_target_pairs={{0,2},{1,3},{2,4},{3,5},{4,6},{5,7},{6,8},{7,9},{8,10},{9,11},{10,... | collective-permute-start | bytes 245768 | tf_op jit(solution)/shard_map/ppermute | solution.py:16
  15.0 13.5 %collective-permute-start = (bf16[128,320]{0,1:T(8,128)(2,1)}, bf16[128,320]{0,1:T(8,128)(2,1)}, u32[]{:S(2)}, u32[]{:S(2)}) collective-permute-start(bf16[128,320]{0,1:T(8,128)(2,1)} %pad_maximum_fusion), channel_id=1, source_target_pairs={{0,1},{1,2},{2,3},{3,4},{4,5},{5,6},{6,7},{7,8},{8,9},{9,10},{10,1... | collective-permute-start | bytes 245768 | tf_op jit(solution)/shard_map/ppermute | solution.py:16
  43.9 9.3 %copy-start.5 = (bf16[32,128]{1,0:T(8,128)(2,1)S(1)}, bf16[32,128]{1,0:T(8,128)(2,1)}, u32[]{:S(2)}) copy-start(bf16[32,128]{1,0:T(8,128)(2,1)} %all_gather.14) | copy-start | bytes 24580
  43.9 38.6 %copy-start.2 = (f32[2048]{0:T(1024)S(1)}, f32[2048]{0:T(1024)}, u32[]{:S(2)}) copy-start(f32[2048]{0:T(1024)} %broadcast.140) | copy-start | bytes 24580
  43.9 38.6 %copy-start.6 = (s32[2048]{0:T(1024)S(1)}, s32[2048]{0:T(1024)}, u32[]{:S(2)}) copy-start(s32[2048]{0:T(1024)} %broadcast_shift-right-logical_fusion) | copy-start | bytes 24580
  82.6 7.1 %copy-start.3 = (s32[2048]{0:T(1024)S(1)}, s32[2048]{0:T(1024)}, u32[]{:S(2)}) copy-start(s32[2048]{0:T(1024)} %get-tuple-element.111) | copy-start | bytes 24580
  82.6 7.1 %copy-start.4 = (s32[2048]{0:T(1024)S(1)}, s32[2048]{0:T(1024)}, u32[]{:S(2)}) copy-start(s32[2048]{0:T(1024)} %get-tuple-element.112) | copy-start | bytes 24580
  82.6 7.1 %copy-start.7 = (s32[640]{0:T(1024)S(1)}, s32[640]{0:T(1024)}, u32[]{:S(2)}) copy-start(s32[640]{0:T(1024)} %iota_add_fusion) | copy-start | bytes 7684
  82.6 7.1 %copy-start.10 = (pred[640]{0:T(1024)(128)(4,1)S(1)}, pred[640]{0:T(1024)(128)(4,1)}, u32[]{:S(2)}) copy-start(pred[640]{0:T(1024)(128)(4,1)} %broadcast_compare_fusion.1) | copy-start | bytes 1924
  93.5 2.7 %copy-start.8 = (f32[2048,1]{0,1:T(1,128)S(1)}, f32[2048,1]{0,1:T(1,128)}, u32[]{:S(2)}) copy-start(f32[2048,1]{0,1:T(1,128)} %get-tuple-element.107) | copy-start | bytes 24580
  93.5 2.7 %copy-start.9 = (f32[2048,1]{0,1:T(1,128)S(1)}, f32[2048,1]{0,1:T(1,128)}, u32[]{:S(2)}) copy-start(f32[2048,1]{0,1:T(1,128)} %get-tuple-element.108) | copy-start | bytes 24580
where the time goes:
time: 102 us; the launch traced here: 101 us
  blocking collectives  45.1 us (44%)
  local copies, waits for them, and re-layouts  16 us (16%)
  starting transfers between devices  15.6 us (15%)
  matrix products  15 us (15%)
  other arithmetic  8.6 us (8%)
    ppermute x4, starting transfers between devices, shifted(): return lax.ppermute(shard, axis, pairs)  15.6 us
    all_gather x1, blocking collectives, local(): lax.all_gather(grouped[0], 'sa', axis=0, tiled=True)  15.2 us
    all_gather x1, blocking collectives, local(): lax.all_gather(grouped[1], 'sa', axis=0, tiled=True)  14.1 us
    unnamed x30, local copies, waits for them, and re-layouts  9.01 us
    all_gather x1, blocking collectives, local(): lax.all_gather(value_summary, 'sb', axis=0, tiled=True)  8.31 us
    all_gather x1, blocking collectives, local(): lax.all_gather(key_summary, 'sb', axis=0, tiled=True)  7.44 us
    dot_general x1, matrix products, local(): jnp.dot(near_weights.astype(jnp.bfloat16), near_values, preferred_element...  4.44 us
    dot_general x2, matrix products, summarize(): jnp.dot(hidden, second, preferred_element_type=jnp.float32)  4.01 us
  transfers between devices with their start and end apart: 4, of which 0 were waited for; matrix products, arithmetic and copies ran while one was open for 24% of the time, Pallas kernels for 0%

commit v1 on v0

v1 whole, which is shorter than its diff:
```python
import functools

import jax
import jax.numpy as jnp
from jax import lax
from jax.experimental import pallas as pl
from jax.experimental.pallas import tpu as pltpu
from jax.sharding import PartitionSpec as P

STRIDE = 16
WINDOW = 512
EXTRA = 16
NEG = -1e30
F32 = jnp.float32
BF16 = jnp.bfloat16


def dot(a, b):
    return jnp.dot(a, b, preferred_element_type=F32)


def silu(x):
    return x / (1.0 + jnp.exp(-x))


def kernel(
    n,
    inner,
    group,
    q_hbm,
    kt_ref,
    v_ref,
    w1k_hbm,
    w2k_ref,
    w1v_hbm,
    w2v_ref,
    table_ref,
    index_ref,
    out_ref,
    q_buf,
    w1k_buf,
    w1v_buf,
    kbuf,
    vbuf,
    gath,
    krows,
    vcols,
    crows,
    ccols,
    near,
    gates,
    out32,
    load_sem,
    halo_send,
    halo_recv,
    sum_send,
    sum_recv,
):
    heads, depth, rows = q_hbm.shape
    dv = v_ref.shape[1]
    reach = WINDOW // rows
    count = rows // STRIDE
    chunk = group * count
    chunks = n // group
    me = lax.axis_index("sa") * inner + lax.axis_index("sb")
    factor = depth ** (-0.5) * 1.4426950408889634

    def place(i):
        return (i // inner, i % inner)

    loads = [
        pltpu.make_async_copy(w1k_hbm, w1k_buf, load_sem.at[0]),
        pltpu.make_async_copy(w1v_hbm, w1v_buf, load_sem.at[1]),
        pltpu.make_async_copy(q_hbm, q_buf.at[:, pl.ds(0, depth), :], load_sem.at[2]),
    ]
    for load in loads:
        load.start()

    barrier = pltpu.get_barrier_semaphore()

    @pl.loop(0, me)
    def _(i):
        pl.semaphore_signal(
            barrier, inc=1, device_id=place(i), device_id_type=pl.DeviceIdType.MESH
        )

    token = lax.broadcasted_iota(jnp.int32, (EXTRA, rows), 1)
    line = lax.broadcasted_iota(jnp.int32, (EXTRA, rows), 0)
    marks = jnp.where((line == 0) | (line - 1 == (token + 1) // STRIDE), 1.0, 0.0).astype(BF16)
    for h in range(heads):
        q_buf[h, depth:, :] = marks
    for i in range(1, reach + 1):

        @pl.when(me < i)
        def _():
            kbuf[i - 1] = jnp.zeros(kbuf.shape[1:], BF16)
            vbuf[i - 1] = jnp.zeros(vbuf.shape[1:], BF16)

    index = index_ref[...]
    for column in range(2):
        gate = jnp.zeros(index.shape, F32)
        for level in range(table_ref.shape[1]):
            gate = jnp.where(index == level, table_ref[column, level], gate)
        gates[column] = gate

    @pl.when(me < n - 1)
    def _():
        pl.semaphore_wait(barrier, n - 1 - me)

    def halo(i):
        to = jnp.minimum(me + i, n - 1)
        return [
            pltpu.make_async_remote_copy(
                src_ref=src,
                dst_ref=dst.at[i - 1],
                send_sem=halo_send.at[part, i - 1],
                recv_sem=halo_recv.at[part, i - 1],
                device_id=place(to),
                device_id_type=pl.DeviceIdType.MESH,
            )
            for part, (src, dst) in enumerate([(kt_ref, kbuf), (v_ref, vbuf)])
        ]

    for i in range(1, reach + 1):

        @pl.when(me + i < n)
        def _():
            for copy in halo(i):
                copy.start()

    @pl.when(me >= 1)
    def _():
        for copy in halo(1):
            copy.wait_recv()

    loads[0].wait()
    own_k = kt_ref[...]
    own_v = v_ref[...]
    lane = lax.broadcasted_iota(jnp.int32, (depth, rows), 1)
    merged = jnp.where(lane >= rows - STRIDE, kbuf[0].astype(F32), own_k.astype(F32))
    front_k = pltpu.roll(merged, STRIDE, 1).astype(BF16)
    zero_k = jnp.zeros_like(own_k)
    spread = [
        jnp.where(lane % STRIDE == u, part, zero_k)
        for part in (front_k, own_k)
        for u in range(STRIDE)
    ]
    sums = dot(w1k_buf[...], jnp.concatenate(spread, axis=0))
    hidden = jnp.sum(sums.T.reshape(count, STRIDE, depth), axis=1)
    key_summary = dot(silu(hidden).astype(BF16), w2k_ref[...])

    loads[1].wait()
    line = lax.broadcasted_iota(jnp.int32, (rows, dv), 0)
    front_v = jnp.concatenate([vbuf[0, rows - STRIDE :, :], own_v[: rows - STRIDE]], axis=0)
    zero_v = jnp.zeros_like(own_v)
    spread = [
        jnp.where(line % STRIDE == u, part, zero_v)
        for part in (front_v, own_v)
        for u in range(STRIDE)
    ]
    sums = dot(jnp.concatenate(spread, axis=1), w1v_buf[...])
    hidden = jnp.sum(sums.reshape(count, STRIDE, dv), axis=1)
    value_summary = dot(silu(hidden).astype(BF16), w2v_ref[...])
    wide = gath.shape[2]
    top = jnp.concatenate([key_summary, jnp.zeros((count, wide - depth), F32)], axis=1)
    bottom = jnp.concatenate([value_summary, jnp.zeros((count, wide - dv), F32)], axis=1)
    gath[me] = jnp.concatenate([top, bottom], axis=0).astype(BF16)

    def summary(source, to):
        return pltpu.make_async_remote_copy(
            src_ref=gath.at[source],
            dst_ref=gath.at[source],
            send_sem=sum_send.at[to],
            recv_sem=sum_recv.at[source],
            device_id=place(to),
            device_id_type=pl.DeviceIdType.MESH,
        )

    @pl.loop(me + 1, n)
    def _(to):
        summary(me, to).start()

    for i in range(2, reach + 1):

        @pl.when(me >= i)
        def _():
            for copy in halo(i):
                copy.wait_recv()

    first_lane = lax.broadcasted_iota(jnp.int32, (rows, EXTRA), 1) == 0
    for slot in range(reach + 1):
        i = reach - slot
        kt = own_k if i == 0 else kbuf[i - 1]
        vv = own_v if i == 0 else vbuf[i - 1]
        here = pl.ds(slot * rows, rows)
        krows[here, :depth] = kt.astype(F32).T.astype(BF16)
        krows[here, depth:] = jnp.where(first_lane & (me < i), NEG, 0.0).astype(BF16)
        vcols[:dv, here] = vv.astype(F32).T.astype(BF16)
    vcols[dv:, :] = jnp.ones((EXTRA, vcols.shape[1]), BF16)
    loads[2].wait()
    pair = 2 * rows
    within = lax.broadcasted_iota(jnp.int32, (rows, pair), 0) <= (
        lax.broadcasted_iota(jnp.int32, (rows, pair), 1) % rows
    )

    def queries(h):
        return jnp.concatenate([q_buf[2 * h], q_buf[2 * h + 1]], axis=1)

    @pl.loop(0, heads // 2)
    def _(h):
        scores = dot(krows[...], queries(h))
        edge = jnp.where(within, scores[reach * rows :], scores[:rows])
        kept = jnp.concatenate([edge, scores[rows : reach * rows]], axis=0)
        best = jnp.max(kept, axis=0, keepdims=True)
        weights = jnp.exp2(kept * factor - best * factor)
        old = jnp.where(within, 0.0, weights[:rows])
        new = jnp.where(within, weights[:rows], 0.0)
        full = jnp.concatenate([old, weights[rows:], new], axis=0).astype(BF16)
        near[h] = dot(vcols[...], full)

    @pl.loop(0, me)
    def _(source):
        summary(source, me).wait_recv()

    needed = me // group + 1

    def prepare(c, carry):
        whole = gath[pl.ds(c * group, group)].astype(F32)
        device = c * group + lax.broadcasted_iota(jnp.int32, (group, 2 * count, wide), 0)
        whole = jnp.where(device <= me, whole, 0.0)
        block = c * chunk + lax.broadcasted_iota(jnp.int32, (chunk, EXTRA), 0)
        column = lax.broadcasted_iota(jnp.int32, (chunk, EXTRA), 1)
        local = block - me * count
        hide = ((column == 0) & (local >= count)) | (
            (column >= 1) & (local >= 0) & (column - 1 <= local)
        )
        here = pl.ds(pl.multiple_of(c * chunk, chunk), chunk)
        crows[here, :depth] = whole[:, :count, :depth].reshape(chunk, depth).astype(BF16)
        crows[here, depth:] = jnp.where(hide, NEG, 0.0).astype(BF16)
        ccols[c, :dv, :] = whole[:, count:, :dv].reshape(chunk, dv).T.astype(BF16)
        ccols[c, dv:, :] = jnp.ones((EXTRA, chunk), BF16)
        return carry

    if chunks == 1:
        prepare(0, 0)
    else:
        lax.fori_loop(0, needed, prepare, 0)

    @pl.loop(0, heads // 2)
    def _(h):
        query = queries(h)

        def part(c):
            here = pl.ds(pl.multiple_of(c * chunk, chunk), chunk)
            scores = dot(crows[here, :], query)
            return scores, jnp.max(scores, axis=0, keepdims=True)

        def weigh(c, scores, best):
            return dot(ccols[c], jnp.exp2(scores * factor - best * factor).astype(BF16))

        if chunks == 1:
            scores, best = part(0)
            far = weigh(0, scores, jnp.maximum(best, 0.1 * NEG))
        else:

            def absorb(c, carry):
                best, total = carry
                scores, fresh = part(c)
                fresh = jnp.maximum(best, fresh)
                shrink = jnp.exp2(best * factor - fresh * factor)
                return fresh, total * shrink + weigh(c, scores, fresh)

            start = (jnp.full((1, pair), 0.1 * NEG, F32), jnp.zeros((dv + EXTRA, pair), F32))
            far = lax.fori_loop(0, needed, absorb, start)[1]
        local = near[h]
        gate = [
            jnp.concatenate([gates[c, pl.ds(2 * h, 1), :], gates[c, pl.ds(2 * h + 1, 1), :]], axis=1)
            for c in range(2)
        ]
        total = far[dv : dv + 1]
        seen = total > 0.0
        far_gate = jnp.where(seen, gate[0] / jnp.where(seen, total, 1.0), 0.0)
        near_gate = gate[1] / local[dv : dv + 1]
        mixed = far[:dv] * far_gate + local[:dv] * near_gate
        for side in range(2):
            out32[pl.ds(2 * h + side, rows, stride=heads), :] = mixed[
                :, side * rows : (side + 1) * rows
            ].T

    out_ref[...] = out32[...].reshape(rows, heads, dv).astype(BF16)

    for i in range(1, reach + 1):

        @pl.when(me + i < n)
        def _():
            for copy in halo(i):
                copy.wait_send()

    @pl.loop(me + 1, n)
    def _(to):
        summary(me, to).wait_send()


def local(
    n,
    inner,
    queries,
    keys,
    values,
    key_first,
    key_second,
    value_first,
    value_second,
    gate_table,
    gate_index,
):
    rows, heads, depth = queries.shape
    dv = values.shape[1]
    reach = WINDOW // rows
    count = rows // STRIDE
    group = min(n, 256 // count)
    chunk = group * count
    wide = 256
    flops = 2 * rows * heads * (depth + dv) * (WINDOW + rows + n * count)
    vmem = pl.BlockSpec(memory_space=pltpu.VMEM)
    hbm = pl.BlockSpec(memory_space=pltpu.HBM)
    smem = pl.BlockSpec(memory_space=pltpu.SMEM)
    return pl.pallas_call(
        functools.partial(kernel, n, inner, group),
        out_shape=jax.ShapeDtypeStruct((rows, heads, dv), BF16),
        in_specs=[hbm, vmem, vmem, hbm, vmem, hbm, vmem, smem, vmem],
        out_specs=vmem,
        scratch_shapes=[
            pltpu.VMEM((heads, depth + EXTRA, rows), BF16),
            pltpu.VMEM(key_first.shape[::-1], BF16),
            pltpu.VMEM(value_first.shape, BF16),
            pltpu.VMEM((reach, depth, rows), BF16),
            pltpu.VMEM((reach, rows, dv), BF16),
            pltpu.VMEM((n, 2 * count, wide), BF16),
            pltpu.VMEM(((reach + 1) * rows, depth + EXTRA), BF16),
            pltpu.VMEM((dv + EXTRA, (reach + 1) * rows), BF16),
            pltpu.VMEM((n * count, depth + EXTRA), BF16),
            pltpu.VMEM((n // group, dv + EXTRA, chunk), BF16),
            pltpu.VMEM((heads // 2, dv + EXTRA, 2 * rows), F32),
            pltpu.VMEM((2, heads, rows), F32),
            pltpu.VMEM((rows * heads, dv), F32),
            pltpu.SemaphoreType.DMA((3,)),
            pltpu.SemaphoreType.DMA((2, reach)),
            pltpu.SemaphoreType.DMA((2, reach)),
            pltpu.SemaphoreType.DMA((n,)),
            pltpu.SemaphoreType.DMA((n,)),
        ],
        compiler_params=pltpu.CompilerParams(
            collective_id=0, has_side_effects=True, vmem_limit_bytes=61440 * 2**10
        ),
        cost_estimate=pl.CostEstimate(
            flops=flops, bytes_accessed=6 * 2**20, transcendentals=rows * heads * 768
        ),
    )(
        queries.transpose(1, 2, 0),
        keys.T,
        values,
        key_first.T,
        key_second,
        value_first,
        value_second,
        gate_table.T,
        gate_index.T,
    )


def solution(mesh):
    split = P(("sa", "sb"))
    inner = mesh.shape["sb"]
    n = mesh.shape["sa"] * inner
    return jax.shard_map(
        functools.partial(local, n, inner),
        mesh=mesh,
        in_specs=(split, split, split, P(), P(), P(), P(), P(), split),
        out_specs=split,
        check_vma=False,
    )
```

time: 102 us -> 27.1 us (0.27)
  the two profiles are of different devices: /device:TPU:0 before, /device:TPU:27 now
where the time goes in v1:
time: 27.1 us; the launch traced here: 26.9 us
  Pallas kernels  25 us (92%)
  local copies, waits for them, and re-layouts  1.87 us (7%)
    pallas_call x1, Pallas kernels, local(): pl.pallas_call(functools.partial(kernel, n, inner, group), out_shape=jax....  25 us
    unnamed x1, local copies, waits for them, and re-layouts  1.87 us

profile of v1, /device:TPU:27, one launch (start us, length us, event | category | flops | bytes accessed | tf_op | source)
XLA Modules:
  0.0 26.9 jit_solution(2981025569627139628)
XLA Ops:
  0.0 25.0 %shard_map.91 = bf16[128,16,128]{2,1,0:T(8,128)(2,1)} custom-call(bf16[16,192,128]{2,1,0:T(8,128)(2,1)} %bitcast.6, bf16[192,128]{1,0:T(8,128)(2,1)} %bitcast.7, bf16[128,128]{1,0:T(8,128)(2,1)} %v_ref.1, bf16[192,6144]{1,0:T(8,128)(2,1)} %bitcast.5, bf16[192,192]{1,0:T(8,128)(2,1)} %w2k_ref.1, bf16[4096,128]{1,0:T(8,128)(2,1)} %w1v_hbm.1, ...), custom_call_target="tpu_custom_call" | custom-call | flops 1174405120 | bytes 6291456 | tf_op jit(solution)/shard_map/pallas_call | solution.py:328
  25.0 1.9 %copy.11 = bf16[128,16,128]{2,1,0:T(8,128)(2,1)} copy(bf16[128,16,128]{2,1,0:T(8,128)(2,1)} %shard_map.91) | data formatting | bytes 1048576

commit v2 on v1

--- a/solution.py
+++ b/solution.py
@@ -55,6 +55,9 @@
     halo_recv,
     sum_send,
     sum_recv,
+    edge_out,
+    edge_in,
+    edge_sem,
 ):
     heads, depth, rows = q_hbm.shape
     dv = v_ref.shape[1]
@@ -96,6 +99,10 @@
             kbuf[i - 1] = jnp.zeros(kbuf.shape[1:], BF16)
             vbuf[i - 1] = jnp.zeros(vbuf.shape[1:], BF16)
 
+    @pl.when(me == 0)
+    def _():
+        edge_in[...] = jnp.zeros(edge_in.shape, F32)
+
     index = index_ref[...]
     for column in range(2):
         gate = jnp.zeros(index.shape, F32)
@@ -103,9 +110,57 @@
             gate = jnp.where(index == level, table_ref[column, level], gate)
         gates[column] = gate
 
+    own_k = kt_ref[...]
+    own_v = v_ref[...]
+    lane = lax.broadcasted_iota(jnp.int32, (depth, rows), 1)
+    zero_k = jnp.zeros_like(own_k)
+    spread = jnp.concatenate(
+        [jnp.where(lane % STRIDE == u, own_k, zero_k) for u in range(STRIDE)], axis=0
+    )
+    loads[0].wait()
+    half = STRIDE * depth
+    front_k, back_k = [
+        jnp.sum(
+            dot(w1k_buf[:, side * half : (side + 1) * half], spread).T.reshape(count, STRIDE, depth),
+            axis=1,
+        )
+        for side in range(2)
+    ]
+    row = lax.broadcasted_iota(jnp.int32, (rows, dv), 0)
+    zero_v = jnp.zeros_like(own_v)
+    spread = jnp.concatenate(
+        [jnp.where(row % STRIDE == u, own_v, zero_v) for u in range(STRIDE)], axis=1
+    )
+    loads[1].wait()
+    half = STRIDE * dv
+    front_v, back_v = [
+        jnp.sum(
+            dot(spread, w1v_buf[side * half : (side + 1) * half, :]).reshape(count, STRIDE, dv),
+            axis=1,
+        )
+        for side in range(2)
+    ]
+    edge_out[:, :depth] = front_k
+    edge_out[:, depth:256] = jnp.zeros((count, 256 - depth), F32)
+    edge_out[:, 256:] = front_v
+
     @pl.when(me < n - 1)
     def _():
         pl.semaphore_wait(barrier, n - 1 - me)
+
+    def edge_copy():
+        return pltpu.make_async_remote_copy(
+            src_ref=edge_out,
+            dst_ref=edge_in,
+            send_sem=edge_sem.at[0],
+            recv_sem=edge_sem.at[1],
+            device_id=place(jnp.minimum(me + 1, n - 1)),
+            device_id_type=pl.DeviceIdType.MESH,
+        )
+
+    @pl.when(me < n - 1)
+    def _():
+        edge_copy().start()
 
     def halo(i):
         to = jnp.minimum(me + i, n - 1)
@@ -130,37 +185,16 @@
 
     @pl.when(me >= 1)
     def _():
-        for copy in halo(1):
-            copy.wait_recv()
-
-    loads[0].wait()
-    own_k = kt_ref[...]
-    own_v = v_ref[...]
-    lane = lax.broadcasted_iota(jnp.int32, (depth, rows), 1)
-    merged = jnp.where(lane >= rows - STRIDE, kbuf[0].astype(F32), own_k.astype(F32))
-    front_k = pltpu.roll(merged, STRIDE, 1).astype(BF16)
-    zero_k = jnp.zeros_like(own_k)
-    spread = [
-        jnp.where(lane % STRIDE == u, part, zero_k)
-        for part in (front_k, own_k)
-        for u in range(STRIDE)
-    ]
-    sums = dot(w1k_buf[...], jnp.concatenate(spread, axis=0))
-    hidden = jnp.sum(sums.T.reshape(count, STRIDE, depth), axis=1)
-    key_summary = dot(silu(hidden).astype(BF16), w2k_ref[...])
-
-    loads[1].wait()
-    line = lax.broadcasted_iota(jnp.int32, (rows, dv), 0)
-    front_v = jnp.concatenate([vbuf[0, rows - STRIDE :, :], own_v[: rows - STRIDE]], axis=0)
-    zero_v = jnp.zeros_like(own_v)
-    spread = [
-        jnp.where(line % STRIDE == u, part, zero_v)
-        for part in (front_v, own_v)
-        for u in range(STRIDE)
-    ]
-    sums = dot(jnp.concatenate(spread, axis=1), w1v_buf[...])
-    hidden = jnp.sum(sums.reshape(count, STRIDE, dv), axis=1)
-    value_summary = dot(silu(hidden).astype(BF16), w2v_ref[...])
+        edge_copy().wait_recv()
+
+    def finish(own, fronts, incoming, second):
+        row = lax.broadcasted_iota(jnp.int32, own.shape, 0)
+        hidden = own + jnp.where(row == 0, pltpu.roll(incoming, 1, 0), pltpu.roll(fronts, 1, 0))
+        return dot(silu(hidden).astype(BF16), second)
+
+    before = edge_in[...]
+    key_summary = finish(back_k, front_k, before[:, :depth], w2k_ref[...])
+    value_summary = finish(back_v, front_v, before[:, 256 : 256 + dv], w2v_ref[...])
     wide = gath.shape[2]
     top = jnp.concatenate([key_summary, jnp.zeros((count, wide - depth), F32)], axis=1)
     bottom = jnp.concatenate([value_summary, jnp.zeros((count, wide - dv), F32)], axis=1)
@@ -180,7 +214,7 @@
     def _(to):
         summary(me, to).start()
 
-    for i in range(2, reach + 1):
+    for i in range(1, reach + 1):
 
         @pl.when(me >= i)
         def _():
@@ -206,7 +240,7 @@
     def queries(h):
         return jnp.concatenate([q_buf[2 * h], q_buf[2 * h + 1]], axis=1)
 
-    @pl.loop(0, heads // 2)
+    @pl.loop(0, heads // 2, unroll=8)
     def _(h):
         scores = dot(krows[...], queries(h))
         edge = jnp.where(within, scores[reach * rows :], scores[:rows])
@@ -246,7 +280,7 @@
     else:
         lax.fori_loop(0, needed, prepare, 0)
 
-    @pl.loop(0, heads // 2)
+    @pl.loop(0, heads // 2, unroll=8)
     def _(h):
         query = queries(h)
 
@@ -295,6 +329,10 @@
         def _():
             for copy in halo(i):
                 copy.wait_send()
+
+    @pl.when(me < n - 1)
+    def _():
+        edge_copy().wait_send()
 
     @pl.loop(me + 1, n)
     def _(to):
@@ -327,7 +365,7 @@
     smem = pl.BlockSpec(memory_space=pltpu.SMEM)
     return pl.pallas_call(
         functools.partial(kernel, n, inner, group),
-        out_shape=jax.ShapeDtypeStruct((rows, heads, dv), BF16),
+        out_shape=pltpu.VMEM((rows, heads, dv), BF16),
         in_specs=[hbm, vmem, vmem, hbm, vmem, hbm, vmem, smem, vmem],
         out_specs=vmem,
         scratch_shapes=[
@@ -349,6 +387,9 @@
             pltpu.SemaphoreType.DMA((2, reach)),
             pltpu.SemaphoreType.DMA((n,)),
             pltpu.SemaphoreType.DMA((n,)),
+            pltpu.VMEM((count, 256 + dv), F32),
+            pltpu.VMEM((count, 256 + dv), F32),
+            pltpu.SemaphoreType.DMA((2,)),
         ],
         compiler_params=pltpu.CompilerParams(
             collective_id=0, has_side_effects=True, vmem_limit_bytes=61440 * 2**10

time: 27.1 us -> 21.5 us (0.79)
  Pallas kernels: 25 us -> 20.3 us
  local copies, waits for them, and re-layouts: 1.87 us -> 0.8 us
    pallas_call x1, Pallas kernels: 25 us -> 20.3 us  [local(): pl.pallas_call(functools.partial(kernel, n, inner, group), out_shape=pltp...]
    unnamed x1, local copies, waits for them, and re-layouts: 1.87 us -> 0.8 us
where the time goes in v2:
time: 21.5 us; the launch traced here: 21.1 us
  Pallas kernels  20.3 us (94%)
  local copies, waits for them, and re-layouts  0.8 us (4%)
    pallas_call x1, Pallas kernels, local(): pl.pallas_call(functools.partial(kernel, n, inner, group), out_shape=pltp...  20.3 us
    unnamed x1, local copies, waits for them, and re-layouts  0.8 us

profile of v2, /device:TPU:27, one launch (start us, length us, event | category | flops | bytes accessed | tf_op | source)
XLA Modules:
  0.0 21.1 jit_solution(14388641717592350139)
XLA Ops:
  0.0 20.3 %shard_map.91 = bf16[128,16,128]{2,1,0:T(8,128)(2,1)S(1)} custom-call(bf16[16,192,128]{2,1,0:T(8,128)(2,1)} %bitcast.6, bf16[192,128]{1,0:T(8,128)(2,1)} %bitcast.7, bf16[128,128]{1,0:T(8,128)(2,1)} %v_ref.1, bf16[192,6144]{1,0:T(8,128)(2,1)} %bitcast.5, bf16[192,192]{1,0:T(8,128)(2,1)} %w2k_ref.1, bf16[4096,128]{1,0:T(8,128)(2,1)} %w1v_hbm.1, ...), custom_call_target="tpu_custom_call" | custom-call | flops 1174405120 | bytes 6291456 | tf_op jit(solution)/shard_map/pallas_call | solution.py:366
  20.3 0.8 %copy.11 = bf16[128,16,128]{2,1,0:T(8,128)(2,1)} copy(bf16[128,16,128]{2,1,0:T(8,128)(2,1)S(1)} %shard_map.91) | data formatting | bytes 1048576
